TPU v7x, 32 devices: a whole 2x2x4 slice. The times are simulated.
32 devices in a mesh: view: 4 (over z), tm: 8 (over y, x, core).
Axes of the slice: x: 2, y: 2, z: 4, core: 2. Of those that a mesh axis runs over, the one named last changes fastest.
Arguments:
- frames: bfloat16 [4, 32, 160, 640], P('view', 'tm'), may hold values from -6 to 6
- ln_gain: float32 [640], replicated, may hold values from 0.1 to 1.9
- w_query: bfloat16 [640, 640], replicated, as said below
- w_key: bfloat16 [640, 640], replicated, as said below
- w_value: bfloat16 [640, 640], replicated, may hold values from -0.25 to 0.25
- w_out: bfloat16 [640, 640], replicated, may hold values from -1 to 1
- conv_gain: float32 [640], replicated, may hold values from 0.1 to 1.9
- conv_weight: bfloat16 [1920, 640], P('tm'), may hold values from -0.25 to 0.25
Outputs:
- block_out: bfloat16 [4, 32, 160, 640], P('view', 'tm')
Inputs may be any that keep to these rules, and one draw needn't show every extreme that they name: `w_query`: a projection matrix. `w_key`: a projection matrix.
All inputs are finite; a program needn't handle non-finite values.
Results may differ from a plain program's by a relative error of at most 0.006.
The roundings to bfloat16 on the way count: a program that leaves them out, or rounds other values in their place, can miss the bound.
Values may be sent and summed in bfloat16 or wider, within the bound.
A program may use at most 64 MiB of HBM per device.

v0:
```python
import jax
import jax.numpy as jnp
from jax import lax
from jax.sharding import PartitionSpec as P

HEADS = 10
HEAD_DIM = 64


def broadcast(shard, axis, root):
    mine = lax.axis_index(axis) == root
    return lax.psum(jnp.where(mine, shard, jnp.zeros_like(shard)), axis)


def shifted_2(block, axis, distance):
    devices = range(lax.axis_size(axis))
    route = [(i - distance, i) for i in devices if i - distance in devices]
    return lax.ppermute(block, axis, route)


def with_halo(shard, sides, width):
    for axis, dim in sides:
        size, length = (lax.axis_size(axis), shard.shape[dim])
        up = [(i, (i + 1) % size) for i in range(size - 1)]
        down = [(j, i) for i, j in up]
        last = lax.slice_in_dim(shard, length - width, length, axis=dim)
        initial = lax.slice_in_dim(shard, 0, width, axis=dim)
        before = lax.ppermute(last, axis, up)
        after = lax.ppermute(initial, axis, down)
        shard = jnp.concatenate([before, shard, after], axis=dim)
    return shard


def layer_norm(values, gain):
    mean = jnp.mean(values, axis=-1, keepdims=True)
    centred = values - mean
    variance = jnp.mean(centred * centred, axis=-1, keepdims=True)
    return centred * lax.rsqrt(variance + 1e-05) * gain


def attend(query, keyset, valueset):
    rows = query.shape[0]
    heads_q = query.reshape(rows, HEADS, HEAD_DIM).transpose(1, 0, 2)
    heads_k = keyset.reshape(keyset.shape[0], HEADS, HEAD_DIM).transpose(1, 0, 2)
    heads_v = valueset.reshape(valueset.shape[0], HEADS, HEAD_DIM).transpose(1, 0, 2)

    def one_head(trio):
        head_q, head_k, head_v = trio
        scores = jnp.dot(head_q, head_k.T, preferred_element_type=jnp.float32) * HEAD_DIM ** (-0.5)
        top = jnp.max(scores, axis=-1, keepdims=True)
        expo = jnp.exp(scores - top)
        weights = (expo / jnp.sum(expo, axis=-1, keepdims=True)).astype(jnp.bfloat16)
        return jnp.dot(weights, head_v, preferred_element_type=jnp.float32)

    outputs = lax.map(one_head, (heads_q, heads_k, heads_v))
    return outputs.transpose(1, 0, 2).reshape(rows, HEADS * HEAD_DIM).astype(jnp.bfloat16)


def project(source, weight):
    return jnp.dot(source, weight, preferred_element_type=jnp.float32).astype(jnp.bfloat16)


def spread_anchor(payload):
    along_row = broadcast(payload, "tm", 0)
    return broadcast(along_row, "view", 0)


def per_device(frames, ln_gain, w_query, w_key, w_value, w_out, conv_gain, conv_weight):
    tokens = frames[0].astype(jnp.float32)
    local_frames = tokens.shape[0]
    frame_tok = tokens.shape[1]
    width = tokens.shape[2]
    normed = layer_norm(tokens, ln_gain).astype(jnp.bfloat16)
    flat = normed.reshape(-1, width)
    query = project(flat, w_query).reshape(local_frames, frame_tok, width)
    own_keys = project(flat, w_key).reshape(local_frames, frame_tok, width)
    own_values = project(flat, w_value).reshape(local_frames, frame_tok, width)
    own_pair = jnp.stack([own_keys, own_values])
    anchor_pair = spread_anchor(own_pair[:, 0])
    shifted = shifted_2(own_pair[:, -1], "tm", 1)
    incoming = jnp.where(lax.axis_index("tm") == 0, own_pair[:, 0], shifted)
    prev_pair = jnp.concatenate([incoming[:, None], own_pair[:, :-1]], axis=1)

    def one_frame(trio):
        frame_q, frame_k, frame_v = trio
        keyset = jnp.concatenate([anchor_pair[0], frame_k], axis=0)
        valueset = jnp.concatenate([anchor_pair[1], frame_v], axis=0)
        return attend(frame_q, keyset, valueset)

    attended = lax.map(one_frame, (query, prev_pair[0], prev_pair[1]))
    mixed = jnp.dot(attended.reshape(-1, width), w_out, preferred_element_type=jnp.float32)
    hidden = (tokens + mixed.reshape(tokens.shape)).astype(jnp.bfloat16)
    activated = jax.nn.silu(layer_norm(hidden.astype(jnp.float32), conv_gain)).astype(jnp.bfloat16)
    padded = with_halo(activated, (("tm", 0),), 1)
    stacked = jnp.concatenate([padded[:-2], padded[1:-1], padded[2:]], axis=-1).reshape(
        -1, 3 * width
    )
    conv = jnp.dot(
        stacked,
        lax.all_gather(conv_weight, "tm", axis=0, tiled=True),
        preferred_element_type=jnp.float32,
    )
    block = (hidden.astype(jnp.float32) + conv.reshape(tokens.shape)).astype(jnp.bfloat16)
    return block[None]


def solution(mesh):
    placed = (P("view", "tm", None, None), P(), P(), P(), P(), P(), P(), P("tm", None))
    return jax.shard_map(
        per_device,
        mesh=mesh,
        in_specs=placed,
        out_specs=P("view", "tm", None, None),
        check_vma=False,
    )
```

profile of v0, /device:TPU:9, one launch (start us, length us, event | category | flops | bytes accessed | tf_op | source)
XLA Modules:
  0.0 192.0 jit_solution(15812592593804419044)
XLA Ops:
  6.6 1.5 convert_reduce_fusion.1
  8.1 1.5 fusion.37
  12.6 3.7 %collective-permute-start = (bf16[2,160,640]{2,1,0:T(8,128)(2,1)S(1)}, bf16[2,160,640]{2,1,0:T(8,128)(2,1)S(1)}, u32[]{:S(2)}, u32[]{:S(2)}) collective-permute-start(bf16[2,160,640]{2,1,0:T(8,128)(2,1)S(1)} %maximum_bitcast_fusion.2), channel_id=1, source_target_pairs={{0,1},{1,2},{2,3},{3,4},{4,5},{5,6},{6,7},{8,9},{9,10},{10,11},{11... | collective-permute-start | bytes 1228808 | tf_op jit(solution)/shard_map/ppermute | solution.py:18
  16.3 4.9 %collective-permute-done = bf16[2,160,640]{2,1,0:T(8,128)(2,1)S(1)} collective-permute-done((bf16[2,160,640]{2,1,0:T(8,128)(2,1)S(1)}, bf16[2,160,640]{2,1,0:T(8,128)(2,1)S(1)}, u32[]{:S(2)}, u32[]{:S(2)}) %collective-permute-start) | collective-permute-done | bytes 409632 | tf_op jit(solution)/shard_map/ppermute | solution.py:18
  22.1 55.5 %all-reduce.3.cloned.1.call-done = bf16[2,160,640]{2,1,0:T(8,128)(2,1)} async-done(((bf16[2,160,640]{2,1,0:T(8,128)(2,1)}), bf16[2,160,640]{2,1,0:T(8,128)(2,1)}) %all-reduce.3.cloned.1.call-update) | async-done | bytes 409616 | tf_op jit(solution)/shard_map/psum | solution.py:12
  79.2 3.1 %convolution_convert_fusion.2 = bf16[640,640]{1,0:T(8,128)(2,1)} fusion(bf16[640,640]{1,0:T(8,128)(2,1)} %copy-done.2, bf16[640,640]{1,0:T(8,128)(2,1)} %param.14), kind=kOutput, calls=%fused_computation.59 | convolution fusion | flops 524697600 | bytes 2457600 | tf_op jit(solution)/shard_map/dot_general | solution.py:60
  82.5 1.3 slice_bitcast_fusion
  83.9 32.2 %all-reduce.5.cloned.1.call-done = bf16[2,160,640]{2,1,0:T(8,128)(2,1)} async-done(((bf16[2,160,640]{2,1,0:T(8,128)(2,1)}), bf16[2,160,640]{2,1,0:T(8,128)(2,1)}) %all-reduce.5.cloned.1.call-update) | async-done | bytes 409616 | tf_op jit(solution)/shard_map/psum | solution.py:12
  116.0 1.2 copy.27
  117.3 47.6 %while.21 = (s32[]{:T(128)}, bf16[4,160,640]{1,2,0:T(8,128)(2,1)}, bf16[4,160,640]{2,1,0:T(8,128)(2,1)}, bf16[2,160,640]{1,2,0:T(8,128)(2,1)S(1)}, bf16[4,160,64...) while((s32[]{:T(128)}, bf16[4,160,640]{1,2,0:T(8,128)(2,1)}, ...), condition=%wide.region_9.10_spmd, body=%wide.region_4.9_spmd.sunk | while | flops 15103684 | bytes 6306402 | solution.py:90
  117.3 1.1 constant_dynamic-slice_fusion.6
  119.1 1.0 constant_dynamic-slice_fusion.5
  120.3 8.1 %while.22 = (s32[]{:T(128)}, bf16[10,160,64]{1,2,0:T(8,128)(2,1)S(1)}, bf16[10,160,64]{1,2,0:T(8,128)(2,1)S(1)}, bf16[10,320,64]{1,2,0:T(8,128)(2,1)S(1)}, bf16[10,320,64]{1,2,0:T(8,128)(2,1)S(1)}, /*index=5*/s32[]{:T(128)}) while((s32[]{:T(128)}, bf16[10,160,64]{1,2,0:T(8,128)(2,1)S(1)}, bf16[10,160,64]{1,2,0:T(8,128)(2,1)S(1)}, ...), condition=%wide.region_8.8_spmd, body=%wide.region_5.7_spmd.sunk | while | flops 13465282 | bytes 858053 | solution.py:55
  129.2 1.1 constant_dynamic-slice_fusion.6
  132.2 8.1 %while.22 = (s32[]{:T(128)}, bf16[10,160,64]{1,2,0:T(8,128)(2,1)S(1)}, bf16[10,160,64]{1,2,0:T(8,128)(2,1)S(1)}, bf16[10,320,64]{1,2,0:T(8,128)(2,1)S(1)}, bf16[10,320,64]{1,2,0:T(8,128)(2,1)S(1)}, /*index=5*/s32[]{:T(128)}) while((s32[]{:T(128)}, bf16[10,160,64]{1,2,0:T(8,128)(2,1)S(1)}, bf16[10,160,64]{1,2,0:T(8,128)(2,1)S(1)}, ...), condition=%wide.region_8.8_spmd, body=%wide.region_5.7_spmd.sunk | while | flops 13465282 | bytes 858053 | solution.py:55
  141.1 1.1 constant_dynamic-slice_fusion.6
  144.1 8.1 %while.22 = (s32[]{:T(128)}, bf16[10,160,64]{1,2,0:T(8,128)(2,1)S(1)}, bf16[10,160,64]{1,2,0:T(8,128)(2,1)S(1)}, bf16[10,320,64]{1,2,0:T(8,128)(2,1)S(1)}, bf16[10,320,64]{1,2,0:T(8,128)(2,1)S(1)}, /*index=5*/s32[]{:T(128)}) while((s32[]{:T(128)}, bf16[10,160,64]{1,2,0:T(8,128)(2,1)S(1)}, bf16[10,160,64]{1,2,0:T(8,128)(2,1)S(1)}, ...), condition=%wide.region_8.8_spmd, body=%wide.region_5.7_spmd.sunk | while | flops 13465282 | bytes 858053 | solution.py:55
  152.9 1.1 constant_dynamic-slice_fusion.6
  155.9 8.1 %while.22 = (s32[]{:T(128)}, bf16[10,160,64]{1,2,0:T(8,128)(2,1)S(1)}, bf16[10,160,64]{1,2,0:T(8,128)(2,1)S(1)}, bf16[10,320,64]{1,2,0:T(8,128)(2,1)S(1)}, bf16[10,320,64]{1,2,0:T(8,128)(2,1)S(1)}, /*index=5*/s32[]{:T(128)}) while((s32[]{:T(128)}, bf16[10,160,64]{1,2,0:T(8,128)(2,1)S(1)}, bf16[10,160,64]{1,2,0:T(8,128)(2,1)S(1)}, ...), condition=%wide.region_8.8_spmd, body=%wide.region_5.7_spmd.sunk | while | flops 13465282 | bytes 858053 | solution.py:55
  164.8 2.7 %convert_reduce_fusion = (f32[4,160]{1,0:T(4,128)S(1)}, bf16[4,160,640]{2,1,0:T(8,128)(2,1)S(1)}) fusion(bf16[4,160,640]{1,2,0:T(8,128)(2,1)} %get-tuple-element.64, bf16[640,640]{1,0:T(8,128)(2,1)S(1)} %copy-done, bf16[1,4,160,640]{3,2,1,0:T(8,128)(2,1)} %param.12), kind=kOutput, calls=%fused_computation.33 | convolution fusion | flops 526335360 | bytes 3279360 | tf_op jit(solution)/shard_map/dot_general | solution.py:91
  168.6 4.9 %collective-permute-start.1 = (bf16[1,160,640]{2,1,0:T(8,128)(2,1)S(1)}, bf16[1,160,640]{2,1,0:T(8,128)(2,1)S(1)}, u32[]{:S(2)}, u32[]{:S(2)}) collective-permute-start(bf16[1,160,640]{2,1,0:T(8,128)(2,1)S(1)} %get-tuple-element.119), channel_id=1, source_target_pairs={{0,1},{1,2},{2,3},{3,4},{4,5},{5,6},{6,7},{8,9},{9,10},{10,11},{11... | collective-permute-start | bytes 614408 | tf_op jit(solution)/shard_map/ppermute | solution.py:28
  173.5 1.9 %collective-permute-start.2 = (bf16[1,160,640]{2,1,0:T(8,128)(2,1)S(1)}, bf16[1,160,640]{2,1,0:T(8,128)(2,1)S(1)}, u32[]{:S(2)}, u32[]{:S(2)}) collective-permute-start(bf16[1,160,640]{2,1,0:T(8,128)(2,1)S(1)} %get-tuple-element.120), channel_id=1, source_target_pairs={{1,0},{2,1},{3,2},{4,3},{5,4},{6,5},{7,6},{9,8},{10,9},{11,10},{12... | collective-permute-start | bytes 614408 | tf_op jit(solution)/shard_map/ppermute | solution.py:29
  176.2 4.4 %collective-permute-done.2 = bf16[1,160,640]{2,1,0:T(8,128)(2,1)S(1)} collective-permute-done((bf16[1,160,640]{2,1,0:T(8,128)(2,1)S(1)}, bf16[1,160,640]{2,1,0:T(8,128)(2,1)S(1)}, u32[]{:S(2)}, u32[]{:S(2)}) %collective-permute-start.2) | collective-permute-done | bytes 204832 | tf_op jit(solution)/shard_map/ppermute | solution.py:29
  180.6 4.8 %fusion.43 = bf16[1,4,160,640]{3,2,1,0:T(8,128)(2,1)} fusion(bf16[1920,640]{1,0:T(8,128)(2,1)} %all-gather.2.cloned.1.call-done, bf16[1,160,640]{2,1,0:T(8,128)(2,1)S(1)} %collective-permute-done.2, bf16[4,160,640]{2,1,0:T(8,128)(2,1)S(1)} %fusion.30, bf16[1,160,640]{2,1,0:T(8,128)(2,1)S(1)} %collective-permute-done.1, ...), kind=kOutput, calls=%fused_computation.60 | convolution fusion | flops 1586380800 | bytes 5324800 | tf_op jit(solution)/shard_map/dot_general | solution.py:98
  (195 shorter events, 49.0 us)
Async XLA Ops:
  6.5 158.3 %copy-start = (bf16[640,640]{1,0:T(8,128)(2,1)S(1)}, bf16[640,640]{1,0:T(8,128)(2,1)}, u32[]{:S(2)}) copy-start(bf16[640,640]{1,0:T(8,128)(2,1)} %param.17) | copy-start | bytes 2457604
  6.5 3.3 %copy-start.1 = (bf16[1,4,160,640]{3,2,1,0:T(8,128)(2,1)S(1)}, bf16[1,4,160,640]{3,2,1,0:T(8,128)(2,1)}, u32[]{:S(2)}) copy-start(bf16[1,4,160,640]{3,2,1,0:T(8,128)(2,1)} %param.12) | copy-start | bytes 2457604
  6.5 3.3 %copy-start.3 = (f32[640]{0:T(1024)S(1)}, f32[640]{0:T(1024)}, u32[]{:S(2)}) copy-start(f32[640]{0:T(1024)} %param.13) | copy-start | bytes 7684
  6.5 3.6 %copy-start.5 = (bf16[640,640]{1,0:T(8,128)(2,1)S(1)}, bf16[640,640]{1,0:T(8,128)(2,1)}, u32[]{:S(2)}) copy-start(bf16[640,640]{1,0:T(8,128)(2,1)} %param.15) | copy-start | bytes 2457604
  6.5 71.0 %all-reduce.3.cloned.1.call-start = ((), (), s32[]{:S(2)}) async-start(), calls=%async_computation | async-start | bytes 819200 | tf_op jit(solution)/shard_map/psum | solution.py:12
  10.2 2.3 %copy-start.2 = (bf16[640,640]{1,0:T(8,128)(2,1)}, bf16[640,640]{1,0:T(8,128)(2,1)S(1)}, u32[]{:S(2)}) copy-start(bf16[640,640]{1,0:T(8,128)(2,1)S(1)} %fusion.35) | copy-start | bytes 2457604
  10.2 1.4 copy-start.6
  12.6 8.6 %collective-permute-start = (bf16[2,160,640]{2,1,0:T(8,128)(2,1)S(1)}, bf16[2,160,640]{2,1,0:T(8,128)(2,1)S(1)}, u32[]{:S(2)}, u32[]{:S(2)}) collective-permute-start(bf16[2,160,640]{2,1,0:T(8,128)(2,1)S(1)} %maximum_bitcast_fusion.2), channel_id=1, source_target_pairs={{0,1},{1,2},{2,3},{3,4},{4,5},{5,6},{6,7},{8,9},{9,10},{10,11},{11... | collective-permute-start | bytes 1228808 | tf_op jit(solution)/shard_map/ppermute | solution.py:18
  22.1 94.0 %all-reduce.5.cloned.1.call-start = ((), (), s32[]{:S(2)}) async-start(), calls=%async_computation.1 | async-start | bytes 819200 | tf_op jit(solution)/shard_map/psum | solution.py:12
  78.4 102.2 %all-gather.2.cloned.1.call-start = ((), (), s32[]{:S(2)}) async-start(), calls=%async_computation.2 | async-start | bytes 2764800 | tf_op jit(solution)/shard_map/all_gather | solution.py:100
  164.8 3.1 %copy-start.4 = (f32[640]{0:T(1024)S(1)}, f32[640]{0:T(1024)}, u32[]{:S(2)}) copy-start(f32[640]{0:T(1024)} %param.18) | copy-start | bytes 7684
  168.6 7.5 %collective-permute-start.1 = (bf16[1,160,640]{2,1,0:T(8,128)(2,1)S(1)}, bf16[1,160,640]{2,1,0:T(8,128)(2,1)S(1)}, u32[]{:S(2)}, u32[]{:S(2)}) collective-permute-start(bf16[1,160,640]{2,1,0:T(8,128)(2,1)S(1)} %get-tuple-element.119), channel_id=1, source_target_pairs={{0,1},{1,2},{2,3},{3,4},{4,5},{5,6},{6,7},{8,9},{9,10},{10,11},{11... | collective-permute-start | bytes 614408 | tf_op jit(solution)/shard_map/ppermute | solution.py:28
  173.5 7.1 %collective-permute-start.2 = (bf16[1,160,640]{2,1,0:T(8,128)(2,1)S(1)}, bf16[1,160,640]{2,1,0:T(8,128)(2,1)S(1)}, u32[]{:S(2)}, u32[]{:S(2)}) collective-permute-start(bf16[1,160,640]{2,1,0:T(8,128)(2,1)S(1)} %get-tuple-element.120), channel_id=1, source_target_pairs={{1,0},{2,1},{3,2},{4,3},{5,4},{6,5},{7,6},{9,8},{10,9},{11,10},{12... | collective-permute-start | bytes 614408 | tf_op jit(solution)/shard_map/ppermute | solution.py:29
Sparse Core Ops, SparseCore 0:
  22.2 55.3 all-reduce.2
  79.9 36.0 all-reduce.4
  118.1 30.9 all-gather.1
where the time goes:
time: 193 us; the launch traced here: 192 us
  waiting for transfers between devices  98.3 us (51%)
  matrix products  35.8 us (19%)
  local copies, waits for them, and re-layouts  16.8 us (9%)
  other arithmetic  16.4 us (8%)
  between operations  13.3 us (7%)
  starting transfers between devices  10.6 us (5%)
    psum x2, waiting for transfers between devices, broadcast(): return lax.psum(jnp.where(mine, shard, jnp.zeros_like(shard)), axis)  87.6 us
    dot_general x40, matrix products, one_head(): jnp.dot(head_q, head_k.T, preferred_element_type=jnp.float32)  12.7 us
    dot_general x40, matrix products, one_head(): return jnp.dot(weights, head_v, preferred_element_type=jnp.float32)  10.7 us
    dynamic_slice x20, local copies, waits for them, and re-layouts, per_device(): attended = lax.map(one_frame, (query, prev_pair[0], prev_pair[1]))  10.2 us
    reduce_sum x40, other arithmetic, one_head(): jnp.sum(expo, axis=-1, keepdims=True)  8.53 us
    dot_general x3, matrix products, project(): jnp.dot(source, weight, preferred_element_type=jnp.float32)  4.91 us
    ppermute x1, waiting for transfers between devices, shifted_2(): return lax.ppermute(block, axis, route)  4.87 us
    ppermute x1, starting transfers between devices, with_halo(): before = lax.ppermute(last, axis, up)  4.86 us
  transfers between devices with their start and end apart: 6, of which 5 were waited for; matrix products, arithmetic and copies ran while one was open for 29% of the time, Pallas kernels for 0%

commit v1 on v0

v1 whole, which is shorter than its diff:
```python
import functools

import jax
import jax.numpy as jnp
from jax import lax
from jax.experimental import pallas as pl
from jax.experimental.pallas import tpu as pltpu
from jax.sharding import PartitionSpec as P

HEAD_DIM = 64
PAIR = 2 * HEAD_DIM
MESH = pl.DeviceIdType.MESH
F32, BF16 = jnp.float32, jnp.bfloat16


def layer_norm(values, gain):
    mean = jnp.mean(values, axis=-1, keepdims=True)
    centred = values - mean
    variance = jnp.mean(centred * centred, axis=-1, keepdims=True)
    return centred * lax.rsqrt(variance + 1e-05) * gain


def mm(a, b):
    return jnp.dot(a, b, preferred_element_type=F32)


def remote(src, dst, send, recv, view, tm):
    return pltpu.make_async_remote_copy(
        src_ref=src, dst_ref=dst, send_sem=send, recv_sem=recv, device_id=(view, tm), device_id_type=MESH
    )


def kernel(nv, nt, pieces, gather,
           fr, ln_gain, wq_h, wk_h, wv_h, wo_h, conv_gain, cw,
           out, x, wq, wk, wv, wo, side, normed, q2, kb, vb, ka, va, att, hid, act, wf,
           load, s1, s2, s3, ra, sp, rp, sw1, rw1, sw2, rw2, sh, rh):
    v, j = lax.axis_index("view"), lax.axis_index("tm")
    nf, tok, width = x.shape
    part = tok // pieces
    shard = cw.shape[0]
    groups = nt // 2
    a, b = j // 2, lax.rem(j, 2)
    sibling = a * 2 + 1 - b
    anc, prev = side.at[0], side.at[1]
    root = (v == 0) & (j == 0)
    holder = (j < pieces) & jnp.logical_not(root)
    other = lax.rem(j + 1, nt)

    loads = [
        pltpu.make_async_copy(fr.at[0], x, load.at[0]),
        pltpu.make_async_copy(wq_h, wq, load.at[1]),
        pltpu.make_async_copy(wk_h, wk, load.at[2]),
        pltpu.make_async_copy(wv_h, wv, load.at[3]),
        pltpu.make_async_copy(wo_h, wo, load.at[4]),
    ]
    for c in loads:
        c.start()
    if gather:
        own_rows = pl.ds(pl.multiple_of(j * shard, 16), shard)
        own_w = pltpu.make_async_copy(cw, wf.at[own_rows], load.at[5])
    else:
        own_w = pltpu.make_async_copy(cw, wf, load.at[5])
    own_w.start()

    barrier = pltpu.get_barrier_semaphore()

    @pl.loop(0, nt)
    def _(t):
        @pl.when(t != j)
        def _():
            pl.semaphore_signal(barrier, inc=1, device_id=(v, t), device_id_type=MESH)

    @pl.loop(0, nv)
    def _(t):
        @pl.when(t != v)
        def _():
            pl.semaphore_signal(barrier, inc=1, device_id=(t, j), device_id_type=MESH)

    pl.semaphore_wait(barrier, nt - 1 + nv - 1)

    def rows(p):
        return pl.ds(pl.multiple_of(p * part, part), part)

    def spread(p, src, act_on):
        @pl.when(v == 0)
        def _():
            @pl.loop(1, nv)
            def _(t):
                act_on(remote(src, anc.at[rows(p)], s2.at[t], ra.at[p], t, j))

        @pl.loop(0, nt)
        def _(t):
            @pl.when((t != j) & ((v != 0) | (t != 0)))
            def _():
                act_on(remote(src, anc.at[rows(p)], s3.at[t], ra.at[p], v, t))

    def scatter(act_on):
        @pl.loop(1, pieces)
        def _(p):
            act_on(remote(fr.at[0, 0, rows(p)], anc.at[rows(p)], s1.at[p], ra.at[p], 0, p))

    def begin(c):
        c.start()

    def sent(c):
        c.wait_send()

    def landed(p):
        remote(anc.at[rows(p)], anc.at[rows(p)], s1.at[p], ra.at[p], v, other).wait_recv()

    def forward():
        landed(j)
        spread(j, anc.at[rows(j)], begin)

    own_anchor = pltpu.make_async_copy(fr.at[0, 0], anc, load.at[6])
    own_prev = pltpu.make_async_copy(fr.at[0, 0], prev, load.at[7])
    to_next = remote(fr.at[0, nf - 1], prev, sp, rp, v, other)

    @pl.when(root)
    def _():
        scatter(begin)
        spread(0, fr.at[0, 0, rows(0)], begin)
        own_anchor.start()

    @pl.when(j < nt - 1)
    def _():
        to_next.start()

    @pl.when(j == 0)
    def _():
        own_prev.start()

    gain = ln_gain[...]
    loads[0].wait()

    @pl.loop(0, nf)
    def _(f):
        normed[pl.ds(pl.multiple_of(f * tok, tok), tok), :] = layer_norm(x[f].astype(F32), gain).astype(BF16)

    @pl.when(holder & (v == 0))
    def _():
        forward()

    lane = lax.broadcasted_iota(jnp.int32, (1, width), 1)
    low = jnp.where(lax.rem(lane, PAIR) < HEAD_DIM, 1.0, 0.0).astype(F32)
    loads[1].wait()
    query = mm(normed[...], wq[...]) * HEAD_DIM ** (-0.5)
    for f in range(nf):
        block = query[f * tok:(f + 1) * tok]
        q2[f, 0:tok, :] = (block * low).astype(BF16)
        q2[f, tok:2 * tok, :] = (block * (1.0 - low)).astype(BF16)
    loads[2].wait()
    loads[3].wait()
    if nf > 1:
        inner = (nf - 1) * tok
        kb[tok:nf * tok, :] = mm(normed[0:inner, :], wk[...]).astype(BF16)
        vb[tok:nf * tok, :] = mm(normed[0:inner, :], wv[...]).astype(BF16)

    @pl.when(holder & (v != 0))
    def _():
        forward()

    def across(act_on):
        @pl.loop(0, groups)
        def _(t):
            @pl.when(t != a)
            def _():
                act_on(remote(cw, wf.at[own_rows], sw1.at[t], rw1.at[a], v, t * 2 + b))

    def shard_rows(t, side_of):
        return pl.ds(pl.multiple_of((t * 2 + side_of) * shard, 16), shard)

    def to_sibling(t):
        return remote(wf.at[shard_rows(t, b)], wf.at[shard_rows(t, b)], sw2.at[t], rw2.at[t], v, sibling)

    if gather:
        across(begin)
        own_w.wait()
        to_sibling(a).start()

    @pl.when(j == 0)
    def _():
        own_prev.wait()

    @pl.when(j > 0)
    def _():
        to_next.wait_recv()

    @pl.when(root)
    def _():
        own_anchor.wait()

    @pl.when(jnp.logical_not(root))
    def _():
        @pl.loop(0, pieces)
        def _(p):
            @pl.when(p != j)
            def _():
                landed(p)

    sides = layer_norm(side[...].astype(F32).reshape(2 * tok, width), gain).astype(BF16)
    keys = mm(sides, wk[...]).astype(BF16)
    values = mm(sides, wv[...]).astype(BF16)
    ka[...] = keys[0:tok]
    va[...] = values[0:tok]
    kb[0:tok, :] = keys[tok:2 * tok]
    vb[0:tok, :] = values[tok:2 * tok]

    loads[4].wait()
    c_gain = conv_gain[...]
    first_half = lax.broadcasted_iota(jnp.int32, (1, PAIR), 1) < HEAD_DIM
    to_right = remote(act.at[pl.ds(nf * tok, tok)], act.at[pl.ds(0, tok)], sh.at[0], rh.at[0], v, other)
    left = lax.rem(j + nt - 1, nt)
    to_left = remote(act.at[pl.ds(tok, tok)], act.at[pl.ds((nf + 1) * tok, tok)], sh.at[1], rh.at[1], v, left)

    @pl.loop(0, nf)
    def _(i):
        f = lax.rem(i + nf - 1, nf)
        if gather:
            @pl.when(i == nf - 1)
            def _():
                @pl.loop(0, groups)
                def _(t):
                    @pl.when(t != a)
                    def _():
                        remote(cw, wf.at[shard_rows(t, b)], sw1.at[t], rw1.at[t], v, other).wait_recv()
                        to_sibling(t).start()

        frame = pl.ds(pl.multiple_of(f * tok, tok), tok)
        for h in range(width // PAIR):
            cols = slice(h * PAIR, (h + 1) * PAIR)
            keyset = jnp.concatenate([ka[:, cols], kb[frame, cols]], axis=0)
            valueset = jnp.concatenate([va[:, cols], vb[frame, cols]], axis=0)
            scores = lax.dot_general(
                q2[f, :, cols], keyset, (((1,), (1,)), ((), ())), preferred_element_type=F32
            )
            expo = jnp.exp(scores - jnp.max(scores, axis=-1, keepdims=True))
            total = jnp.sum(expo, axis=-1, keepdims=True)
            mixed = mm(expo.astype(BF16), valueset) / total
            att[:, cols] = jnp.where(first_half, mixed[0:tok], mixed[tok:2 * tok]).astype(BF16)
        hidden = (x[f].astype(F32) + mm(att[...], wo[...])).astype(BF16)
        hid[frame, :] = hidden
        normal = layer_norm(hidden.astype(F32), c_gain)
        act[pl.ds(pl.multiple_of((f + 1) * tok, tok), tok), :] = (normal * jax.nn.sigmoid(normal)).astype(BF16)

        @pl.when((i == 0) & (j < nt - 1))
        def _():
            to_right.start()

        @pl.when((f == 0) & (j > 0))
        def _():
            to_left.start()

    @pl.when(j == 0)
    def _():
        act[0:tok, :] = jnp.zeros((tok, width), BF16)

    @pl.when(j > 0)
    def _():
        to_right.wait_recv()

    @pl.when(j == nt - 1)
    def _():
        act[(nf + 1) * tok:(nf + 2) * tok, :] = jnp.zeros((tok, width), BF16)

    @pl.when(j < nt - 1)
    def _():
        to_left.wait_recv()

    if gather:
        @pl.loop(0, groups)
        def _(t):
            remote(cw, wf.at[shard_rows(t, 1 - b)], sw2.at[t], rw2.at[t], v, other).wait_recv()
    else:
        own_w.wait()

    total = hid[...].astype(F32)
    for tap in range(3):
        total += mm(act[tap * tok:(tap + nf) * tok, :], wf[tap * width:(tap + 1) * width, :])
    out[...] = total.astype(BF16).reshape(out.shape)

    @pl.when(root)
    def _():
        scatter(sent)
        spread(0, fr.at[0, 0, rows(0)], sent)

    @pl.when(holder)
    def _():
        spread(j, anc.at[rows(j)], sent)

    @pl.when(j < nt - 1)
    def _():
        to_next.wait_send()
        to_right.wait_send()

    @pl.when(j > 0)
    def _():
        to_left.wait_send()

    if gather:
        across(sent)

        @pl.loop(0, groups)
        def _(t):
            to_sibling(t).wait_send()


def solution(mesh):
    nv, nt = mesh.shape["view"], mesh.shape["tm"]

    def per_device(frames, ln_gain, w_query, w_key, w_value, w_out, conv_gain, conv_weight):
        _, nf, tok, width = frames.shape
        shard = conv_weight.shape[0]
        gather = nt % 2 == 0 and shard % 16 == 0
        if not gather:
            conv_weight = lax.all_gather(conv_weight, "tm", axis=0, tiled=True)
        pieces = max(n for n in range(1, nt + 1) if tok % (16 * n) == 0)
        anywhere = pl.BlockSpec(memory_space=pl.ANY)
        vmem = pl.BlockSpec(memory_space=pltpu.VMEM)
        square = pltpu.VMEM((width, width), BF16)
        dma = pltpu.SemaphoreType.DMA
        return pl.pallas_call(
            functools.partial(kernel, nv, nt, pieces, gather),
            out_shape=jax.ShapeDtypeStruct(frames.shape, BF16),
            in_specs=[anywhere, vmem, anywhere, anywhere, anywhere, anywhere, vmem, anywhere],
            out_specs=vmem,
            scratch_shapes=[
                pltpu.VMEM((nf, tok, width), BF16),
                square, square, square, square,
                pltpu.VMEM((2, tok, width), BF16),
                pltpu.VMEM((nf * tok, width), BF16),
                pltpu.VMEM((nf, 2 * tok, width), BF16),
                pltpu.VMEM((nf * tok, width), BF16),
                pltpu.VMEM((nf * tok, width), BF16),
                pltpu.VMEM((tok, width), BF16),
                pltpu.VMEM((tok, width), BF16),
                pltpu.VMEM((tok, width), BF16),
                pltpu.VMEM((nf * tok, width), BF16),
                pltpu.VMEM(((nf + 2) * tok, width), BF16),
                pltpu.VMEM((3 * width, width), BF16),
                dma((8,)), dma((pieces,)), dma((nv,)), dma((nt,)), dma((pieces,)),
                dma, dma,
                dma((nt,)), dma((nt,)), dma((nt,)), dma((nt,)), dma((2,)), dma((2,)),
            ],
            compiler_params=pltpu.CompilerParams(
                collective_id=0, has_side_effects=True, vmem_limit_bytes=60 * 1024 * 1024
            ),
        )(frames, ln_gain[None], w_query, w_key, w_value, w_out, conv_gain[None], conv_weight)

    placed = (P("view", "tm", None, None), P(), P(), P(), P(), P(), P(), P("tm", None))
    return jax.shard_map(
        per_device, mesh=mesh, in_specs=placed, out_specs=P("view", "tm", None, None), check_vma=False
    )
```

time: 193 us -> 43.2 us (0.22)
  the two profiles are of different devices: /device:TPU:9 before, /device:TPU:25 now
where the time goes in v1:
time: 43.2 us; the launch traced here: 43 us
  Pallas kernels  39 us (90%)
  local copies, waits for them, and re-layouts  3.96 us (9%)
    pallas_call x1, Pallas kernels, per_device(): pl.pallas_call(functools.partial(kernel, nv, nt, pieces, gather), out_sha...  39 us
    unnamed x3, local copies, waits for them, and re-layouts  2.11 us
    broadcast_in_dim x1, local copies, waits for them, and re-layouts, per_device(): ln_gain[None]  1.28 us

profile of v1, /device:TPU:25, one launch (start us, length us, event | category | flops | bytes accessed | tf_op | source)
XLA Modules:
  0.0 43.0 jit_solution(2795916882671065330)
XLA Ops:
  0.0 0.0 copy-start
  0.0 1.3 %broadcast_in_dim.6.ln_gain = f32[1,640]{1,0:T(1,128)} reshape(f32[640]{0:T(1024)} %param.9) | data formatting | bytes 5120 | tf_op jit(solution)/shard_map/broadcast_in_dim | solution.py:348
  1.3 0.0 copy-done
  1.3 0.6 %broadcast_in_dim.7.conv_gain = f32[1,640]{1,0:T(1,128)} reshape(f32[640]{0:T(1024)S(1)} %copy-done) | data formatting | bytes 5120 | tf_op jit(solution)/shard_map/broadcast_in_dim | solution.py:348
  1.9 39.0 %shard_map.82 = bf16[1,4,160,640]{3,2,1,0:T(8,128)(2,1)} custom-call(bf16[1,4,160,640]{3,2,1,0:T(8,128)(2,1)} %fr.1, f32[1,640]{1,0:T(1,128)} %broadcast_in_dim.6.ln_gain, bf16[640,640]{1,0:T(8,128)(2,1)} %wq_h.1, bf16[640,640]{1,0:T(8,128)(2,1)} %wk_h.1, bf16[640,640]{1,0:T(8,128)(2,1)} %wv_h.1, bf16[640,640]{1,0:T(8,128)(2,1)} %wo_h.1, ...), custom_call_target="tpu_custom_call" | custom-call | tf_op jit(solution)/shard_map/pallas_call | solution.py:322
  40.9 2.1 %copy.10 = bf16[1,4,160,640]{3,2,1,0:T(8,128)(2,1)} copy(bf16[1,4,160,640]{3,2,1,0:T(8,128)(2,1)} %shard_map.82) | data formatting | bytes 1638400
Async XLA Ops:
  0.0 1.3 %copy-start = (f32[640]{0:T(1024)S(1)}, f32[640]{0:T(1024)}, u32[]{:S(2)}) copy-start(f32[640]{0:T(1024)} %param.14) | copy-start | bytes 7684

commit v2 on v1

--- a/solution.py
+++ b/solution.py
@@ -130,7 +130,7 @@
     def _():
         own_prev.start()
 
-    gain = ln_gain[...]
+    gain = ln_gain[...].reshape(1, width)
     loads[0].wait()
 
     @pl.loop(0, nf)
@@ -140,6 +140,23 @@
     @pl.when(holder & (v == 0))
     def _():
         forward()
+
+    def across(act_on):
+        @pl.loop(1, groups)
+        def _(d):
+            t = lax.rem(a + groups - d, groups)
+            act_on(remote(cw, wf.at[own_rows], sw1.at[t], rw1.at[a], v, t * 2 + b))
+
+    def shard_rows(t, side_of):
+        return pl.ds(pl.multiple_of((t * 2 + side_of) * shard, 16), shard)
+
+    def to_sibling(t):
+        return remote(wf.at[shard_rows(t, b)], wf.at[shard_rows(t, b)], sw2.at[t], rw2.at[t], v, sibling)
+
+    if gather:
+        across(begin)
+        own_w.wait()
+        to_sibling(a).start()
 
     lane = lax.broadcasted_iota(jnp.int32, (1, width), 1)
     low = jnp.where(lax.rem(lane, PAIR) < HEAD_DIM, 1.0, 0.0).astype(F32)
@@ -160,24 +177,6 @@
     def _():
         forward()
 
-    def across(act_on):
-        @pl.loop(0, groups)
-        def _(t):
-            @pl.when(t != a)
-            def _():
-                act_on(remote(cw, wf.at[own_rows], sw1.at[t], rw1.at[a], v, t * 2 + b))
-
-    def shard_rows(t, side_of):
-        return pl.ds(pl.multiple_of((t * 2 + side_of) * shard, 16), shard)
-
-    def to_sibling(t):
-        return remote(wf.at[shard_rows(t, b)], wf.at[shard_rows(t, b)], sw2.at[t], rw2.at[t], v, sibling)
-
-    if gather:
-        across(begin)
-        own_w.wait()
-        to_sibling(a).start()
-
     @pl.when(j == 0)
     def _():
         own_prev.wait()
@@ -207,7 +206,8 @@
     vb[0:tok, :] = values[tok:2 * tok]
 
     loads[4].wait()
-    c_gain = conv_gain[...]
+    c_gain = conv_gain[...].reshape(1, width)
+    ones = jnp.ones((2 * tok, PAIR), BF16)
     first_half = lax.broadcasted_iota(jnp.int32, (1, PAIR), 1) < HEAD_DIM
     to_right = remote(act.at[pl.ds(nf * tok, tok)], act.at[pl.ds(0, tok)], sh.at[0], rh.at[0], v, other)
     left = lax.rem(j + nt - 1, nt)
@@ -217,14 +217,13 @@
     def _(i):
         f = lax.rem(i + nf - 1, nf)
         if gather:
-            @pl.when(i == nf - 1)
-            def _():
-                @pl.loop(0, groups)
-                def _(t):
-                    @pl.when(t != a)
-                    def _():
-                        remote(cw, wf.at[shard_rows(t, b)], sw1.at[t], rw1.at[t], v, other).wait_recv()
-                        to_sibling(t).start()
+            @pl.loop(1, groups)
+            def _(d):
+                @pl.when(i == d * nf // groups)
+                def _():
+                    t = lax.rem(a + d, groups)
+                    remote(cw, wf.at[shard_rows(t, b)], sw1.at[t], rw1.at[t], v, other).wait_recv()
+                    to_sibling(t).start()
 
         frame = pl.ds(pl.multiple_of(f * tok, tok), tok)
         for h in range(width // PAIR):
@@ -235,8 +234,8 @@
                 q2[f, :, cols], keyset, (((1,), (1,)), ((), ())), preferred_element_type=F32
             )
             expo = jnp.exp(scores - jnp.max(scores, axis=-1, keepdims=True))
-            total = jnp.sum(expo, axis=-1, keepdims=True)
-            mixed = mm(expo.astype(BF16), valueset) / total
+            summed = mm(expo.astype(BF16), jnp.concatenate([valueset, ones], axis=1))
+            mixed = summed[:, 0:PAIR] / summed[:, PAIR:2 * PAIR]
             att[:, cols] = jnp.where(first_half, mixed[0:tok], mixed[tok:2 * tok]).astype(BF16)
         hidden = (x[f].astype(F32) + mm(att[...], wo[...])).astype(BF16)
         hid[frame, :] = hidden
@@ -303,6 +302,14 @@
         @pl.loop(0, groups)
         def _(t):
             to_sibling(t).wait_send()
+
+
+def hand_over(src, out, done):
+    copies = [pltpu.make_async_copy(src.at[0, f], out.at[0, f], done.at[f]) for f in range(src.shape[1])]
+    for c in copies:
+        c.start()
+    for c in copies:
+        c.wait()
 
 
 def solution(mesh):
@@ -315,13 +322,13 @@
         if not gather:
             conv_weight = lax.all_gather(conv_weight, "tm", axis=0, tiled=True)
         pieces = max(n for n in range(1, nt + 1) if tok % (16 * n) == 0)
-        anywhere = pl.BlockSpec(memory_space=pl.ANY)
+        anywhere = pl.BlockSpec(memory_space=pltpu.HBM)
         vmem = pl.BlockSpec(memory_space=pltpu.VMEM)
         square = pltpu.VMEM((width, width), BF16)
         dma = pltpu.SemaphoreType.DMA
-        return pl.pallas_call(
+        block = pl.pallas_call(
             functools.partial(kernel, nv, nt, pieces, gather),
-            out_shape=jax.ShapeDtypeStruct(frames.shape, BF16),
+            out_shape=pltpu.VMEM(frames.shape, BF16),
             in_specs=[anywhere, vmem, anywhere, anywhere, anywhere, anywhere, vmem, anywhere],
             out_specs=vmem,
             scratch_shapes=[
@@ -343,9 +350,16 @@
                 dma((nt,)), dma((nt,)), dma((nt,)), dma((nt,)), dma((2,)), dma((2,)),
             ],
             compiler_params=pltpu.CompilerParams(
-                collective_id=0, has_side_effects=True, vmem_limit_bytes=60 * 1024 * 1024
+                collective_id=0, has_side_effects=True, vmem_limit_bytes=48 * 1024 * 1024
             ),
-        )(frames, ln_gain[None], w_query, w_key, w_value, w_out, conv_gain[None], conv_weight)
+        )(frames, ln_gain, w_query, w_key, w_value, w_out, conv_gain, conv_weight)
+        return pl.pallas_call(
+            hand_over,
+            out_shape=jax.ShapeDtypeStruct(frames.shape, BF16),
+            in_specs=[vmem],
+            out_specs=anywhere,
+            scratch_shapes=[dma((nf,))],
+        )(block)
 
     placed = (P("view", "tm", None, None), P(), P(), P(), P(), P(), P(), P("tm", None))
     return jax.shard_map(

time: 43.2 us -> 48.2 us (1.12)
  the two profiles are of different devices: /device:TPU:25 before, /device:TPU:11 now
where the time goes in v2:
time: 48.2 us; the launch traced here: 47.8 us
  Pallas kernels  38.8 us (80%)
  local copies, waits for them, and re-layouts  8.94 us (19%)
    pallas_call x1, Pallas kernels, per_device(): pl.pallas_call(functools.partial(kernel, nv, nt, pieces, gather), out_sha...  36.8 us
    unnamed x18, local copies, waits for them, and re-layouts  8.94 us
    pallas_call x1, Pallas kernels, per_device(): pl.pallas_call(hand_over, out_shape=jax.ShapeDtypeStruct(frames.shape, BF...  2.06 us

profile of v2, /device:TPU:11, one launch (start us, length us, event | category | flops | bytes accessed | tf_op | source)
XLA Modules:
  0.0 47.8 jit_solution(4697583818252381564)
XLA Ops:
  0.0 0.0 copy-start.1
  0.0 1.1 %copy-done.1 = bf16[1,4,160,640]{3,2,1,0:T(8,128)(2,1)S(1)} copy-done((bf16[1,4,160,640]{3,2,1,0:T(8,128)(2,1)S(1)}, bf16[1,4,160,640]{3,2,1,0:T(8,128)(2,1)}, u32[]{:S(2)}) %copy-start.1) | copy-done | bytes 819224
  1.1 0.0 copy-start.2
  1.1 1.1 %copy-done.2 = bf16[640,640]{1,0:T(8,128)(2,1)S(1)} copy-done((bf16[640,640]{1,0:T(8,128)(2,1)S(1)}, bf16[640,640]{1,0:T(8,128)(2,1)}, u32[]{:S(2)}) %copy-start.2) | copy-done | bytes 819224
  2.3 0.0 copy-start.3
  2.3 1.1 %copy-done.3 = bf16[640,640]{1,0:T(8,128)(2,1)S(1)} copy-done((bf16[640,640]{1,0:T(8,128)(2,1)S(1)}, bf16[640,640]{1,0:T(8,128)(2,1)}, u32[]{:S(2)}) %copy-start.3) | copy-done | bytes 819224
  3.4 0.0 copy-start.4
  3.4 1.1 %copy-done.4 = bf16[640,640]{1,0:T(8,128)(2,1)S(1)} copy-done((bf16[640,640]{1,0:T(8,128)(2,1)S(1)}, bf16[640,640]{1,0:T(8,128)(2,1)}, u32[]{:S(2)}) %copy-start.4) | copy-done | bytes 819224
  4.6 0.0 copy-start.5
  4.6 1.1 %copy-done.5 = bf16[640,640]{1,0:T(8,128)(2,1)S(1)} copy-done((bf16[640,640]{1,0:T(8,128)(2,1)S(1)}, bf16[640,640]{1,0:T(8,128)(2,1)}, u32[]{:S(2)}) %copy-start.5) | copy-done | bytes 819224
  5.7 0.0 copy-start.6
  5.7 1.0 %copy-done.6 = bf16[240,640]{1,0:T(8,128)(2,1)S(1)} copy-done((bf16[240,640]{1,0:T(8,128)(2,1)S(1)}, bf16[240,640]{1,0:T(8,128)(2,1)}, u32[]{:S(2)}) %copy-start.6) | copy-done | bytes 307224
  6.7 0.0 copy-start.7
  6.7 0.7 %copy-done.7 = f32[640]{0:T(1024)S(1)} copy-done((f32[640]{0:T(1024)S(1)}, f32[640]{0:T(1024)}, u32[]{:S(2)}) %copy-start.7) | copy-done | bytes 2584
  7.4 0.0 copy-start.8
  7.4 0.7 %copy-done.8 = f32[640]{0:T(1024)S(1)} copy-done((f32[640]{0:T(1024)S(1)}, f32[640]{0:T(1024)}, u32[]{:S(2)}) %copy-start.8) | copy-done | bytes 2584
  8.1 36.8 %shard_map.82.src = bf16[1,4,160,640]{3,2,1,0:T(8,128)(2,1)S(1)} custom-call(bf16[1,4,160,640]{3,2,1,0:T(8,128)(2,1)S(1)} %copy-done.1, f32[640]{0:T(1024)S(1)} %copy-done.7, bf16[640,640]{1,0:T(8,128)(2,1)S(1)} %copy-done.2, bf16[640,640]{1,0:T(8,128)(2,1)S(1)} %copy-done.3, bf16[640,640]{1,0:T(8,128)(2,1)S(1)} %copy-done.4, ...), custom_call_target="tpu_custom_call" | custom-call | tf_op jit(solution)/shard_map/pallas_call | solution.py:329
  44.8 0.0 copy-start
  44.8 0.9 %copy-done = bf16[1,4,160,640]{3,2,1,0:T(8,128)(2,1)} copy-done((bf16[1,4,160,640]{3,2,1,0:T(8,128)(2,1)}, bf16[1,4,160,640]{3,2,1,0:T(8,128)(2,1)S(1)}, u32[]{:S(2)}) %copy-start) | copy-done | bytes 819224
  45.7 2.1 %shard_map.83 = bf16[1,4,160,640]{3,2,1,0:T(8,128)(2,1)} custom-call(bf16[1,4,160,640]{3,2,1,0:T(8,128)(2,1)} %copy-done), custom_call_target="tpu_custom_call" | custom-call | tf_op jit(solution)/shard_map/pallas_call | solution.py:356
Async XLA Ops:
  0.0 1.1 %copy-start.1 = (bf16[1,4,160,640]{3,2,1,0:T(8,128)(2,1)S(1)}, bf16[1,4,160,640]{3,2,1,0:T(8,128)(2,1)}, u32[]{:S(2)}) copy-start(bf16[1,4,160,640]{3,2,1,0:T(8,128)(2,1)} %fr.1) | copy-start | bytes 2457604
  1.1 1.1 %copy-start.2 = (bf16[640,640]{1,0:T(8,128)(2,1)S(1)}, bf16[640,640]{1,0:T(8,128)(2,1)}, u32[]{:S(2)}) copy-start(bf16[640,640]{1,0:T(8,128)(2,1)} %wq_h.1) | copy-start | bytes 2457604
  2.3 1.1 %copy-start.3 = (bf16[640,640]{1,0:T(8,128)(2,1)S(1)}, bf16[640,640]{1,0:T(8,128)(2,1)}, u32[]{:S(2)}) copy-start(bf16[640,640]{1,0:T(8,128)(2,1)} %wk_h.1) | copy-start | bytes 2457604
  3.4 1.1 %copy-start.4 = (bf16[640,640]{1,0:T(8,128)(2,1)S(1)}, bf16[640,640]{1,0:T(8,128)(2,1)}, u32[]{:S(2)}) copy-start(bf16[640,640]{1,0:T(8,128)(2,1)} %wv_h.1) | copy-start | bytes 2457604
  4.6 1.1 %copy-start.5 = (bf16[640,640]{1,0:T(8,128)(2,1)S(1)}, bf16[640,640]{1,0:T(8,128)(2,1)}, u32[]{:S(2)}) copy-start(bf16[640,640]{1,0:T(8,128)(2,1)} %wo_h.1) | copy-start | bytes 2457604
  5.7 1.0 %copy-start.6 = (bf16[240,640]{1,0:T(8,128)(2,1)S(1)}, bf16[240,640]{1,0:T(8,128)(2,1)}, u32[]{:S(2)}) copy-start(bf16[240,640]{1,0:T(8,128)(2,1)} %cw.1) | copy-start | bytes 921604
  6.7 0.7 %copy-start.7 = (f32[640]{0:T(1024)S(1)}, f32[640]{0:T(1024)}, u32[]{:S(2)}) copy-start(f32[640]{0:T(1024)} %ln_gain.1) | copy-start | bytes 7684
  7.4 0.7 %copy-start.8 = (f32[640]{0:T(1024)S(1)}, f32[640]{0:T(1024)}, u32[]{:S(2)}) copy-start(f32[640]{0:T(1024)} %conv_gain.1) | copy-start | bytes 7684
  44.8 0.9 %copy-start = (bf16[1,4,160,640]{3,2,1,0:T(8,128)(2,1)}, bf16[1,4,160,640]{3,2,1,0:T(8,128)(2,1)S(1)}, u32[]{:S(2)}) copy-start(bf16[1,4,160,640]{3,2,1,0:T(8,128)(2,1)S(1)} %shard_map.82.src) | copy-start | bytes 2457604

commit v3 on v2

--- a/solution.py
+++ b/solution.py
@@ -31,9 +31,9 @@
 
 
 def kernel(nv, nt, pieces, gather,
-           fr, ln_gain, wq_h, wk_h, wv_h, wo_h, conv_gain, cw,
-           out, x, wq, wk, wv, wo, side, normed, q2, kb, vb, ka, va, att, hid, act, wf,
-           load, s1, s2, s3, ra, sp, rp, sw1, rw1, sw2, rw2, sh, rh):
+           fr, ln_gain_h, wq_h, wk_h, wv_h, wo_h, conv_gain_h, cw,
+           out, x, wq, wk, wv, wo, side, normed, q2, kb, vb, ka, va, att, hid, act, wf, ln_gain, conv_gain,
+           load, s1, s3, ra, sp, rp, sw1, rw1, sw2, rw2, sh, rh):
     v, j = lax.axis_index("view"), lax.axis_index("tm")
     nf, tok, width = x.shape
     part = tok // pieces
@@ -52,6 +52,8 @@
         pltpu.make_async_copy(wk_h, wk, load.at[2]),
         pltpu.make_async_copy(wv_h, wv, load.at[3]),
         pltpu.make_async_copy(wo_h, wo, load.at[4]),
+        pltpu.make_async_copy(ln_gain_h, ln_gain, load.at[8]),
+        pltpu.make_async_copy(conv_gain_h, conv_gain, load.at[9]),
     ]
     for c in loads:
         c.start()
@@ -70,24 +72,36 @@
         def _():
             pl.semaphore_signal(barrier, inc=1, device_id=(v, t), device_id_type=MESH)
 
-    @pl.loop(0, nv)
-    def _(t):
-        @pl.when(t != v)
-        def _():
-            pl.semaphore_signal(barrier, inc=1, device_id=(t, j), device_id_type=MESH)
-
-    pl.semaphore_wait(barrier, nt - 1 + nv - 1)
+    @pl.when((v > 0) & (j < pieces))
+    def _():
+        pl.semaphore_signal(barrier, inc=1, device_id=(0, 0), device_id_type=MESH)
+
+    @pl.when(root)
+    def _():
+        @pl.loop(1, nv)
+        def _(t):
+            @pl.loop(0, pieces)
+            def _(p):
+                pl.semaphore_signal(barrier, inc=1, device_id=(t, p), device_id_type=MESH)
+
+    far_holder = (v > 0) & (j < pieces)
+
+    @pl.when(root)
+    def _():
+        pl.semaphore_wait(barrier, nt - 1 + (nv - 1) * pieces)
+
+    @pl.when(far_holder)
+    def _():
+        pl.semaphore_wait(barrier, nt)
+
+    @pl.when(jnp.logical_not(root | far_holder))
+    def _():
+        pl.semaphore_wait(barrier, nt - 1)
 
     def rows(p):
         return pl.ds(pl.multiple_of(p * part, part), part)
 
     def spread(p, src, act_on):
-        @pl.when(v == 0)
-        def _():
-            @pl.loop(1, nv)
-            def _(t):
-                act_on(remote(src, anc.at[rows(p)], s2.at[t], ra.at[p], t, j))
-
         @pl.loop(0, nt)
         def _(t):
             @pl.when((t != j) & ((v != 0) | (t != 0)))
@@ -95,9 +109,15 @@
                 act_on(remote(src, anc.at[rows(p)], s3.at[t], ra.at[p], v, t))
 
     def scatter(act_on):
-        @pl.loop(1, pieces)
-        def _(p):
-            act_on(remote(fr.at[0, 0, rows(p)], anc.at[rows(p)], s1.at[p], ra.at[p], 0, p))
+        @pl.loop(0, nv)
+        def _(back):
+            t = nv - 1 - back
+
+            @pl.loop(0, pieces)
+            def _(p):
+                @pl.when((t != 0) | (p != 0))
+                def _():
+                    act_on(remote(fr.at[0, 0, rows(p)], anc.at[rows(p)], s1.at[t, p], ra.at[p], t, p))
 
     def begin(c):
         c.start()
@@ -106,7 +126,7 @@
         c.wait_send()
 
     def landed(p):
-        remote(anc.at[rows(p)], anc.at[rows(p)], s1.at[p], ra.at[p], v, other).wait_recv()
+        remote(anc.at[rows(p)], anc.at[rows(p)], s3.at[0], ra.at[p], v, other).wait_recv()
 
     def forward():
         landed(j)
@@ -130,16 +150,13 @@
     def _():
         own_prev.start()
 
+    loads[0].wait()
+    loads[5].wait()
     gain = ln_gain[...].reshape(1, width)
-    loads[0].wait()
 
     @pl.loop(0, nf)
     def _(f):
         normed[pl.ds(pl.multiple_of(f * tok, tok), tok), :] = layer_norm(x[f].astype(F32), gain).astype(BF16)
-
-    @pl.when(holder & (v == 0))
-    def _():
-        forward()
 
     def across(act_on):
         @pl.loop(1, groups)
@@ -152,11 +169,6 @@
 
     def to_sibling(t):
         return remote(wf.at[shard_rows(t, b)], wf.at[shard_rows(t, b)], sw2.at[t], rw2.at[t], v, sibling)
-
-    if gather:
-        across(begin)
-        own_w.wait()
-        to_sibling(a).start()
 
     lane = lax.broadcasted_iota(jnp.int32, (1, width), 1)
     low = jnp.where(lax.rem(lane, PAIR) < HEAD_DIM, 1.0, 0.0).astype(F32)
@@ -166,6 +178,16 @@
         block = query[f * tok:(f + 1) * tok]
         q2[f, 0:tok, :] = (block * low).astype(BF16)
         q2[f, tok:2 * tok, :] = (block * (1.0 - low)).astype(BF16)
+
+    @pl.when(holder)
+    def _():
+        forward()
+
+    if gather:
+        across(begin)
+        own_w.wait()
+        to_sibling(a).start()
+
     loads[2].wait()
     loads[3].wait()
     if nf > 1:
@@ -173,10 +195,6 @@
         kb[tok:nf * tok, :] = mm(normed[0:inner, :], wk[...]).astype(BF16)
         vb[tok:nf * tok, :] = mm(normed[0:inner, :], wv[...]).astype(BF16)
 
-    @pl.when(holder & (v != 0))
-    def _():
-        forward()
-
     @pl.when(j == 0)
     def _():
         own_prev.wait()
@@ -184,6 +202,12 @@
     @pl.when(j > 0)
     def _():
         to_next.wait_recv()
+
+    def projected(frame):
+        frame = layer_norm(frame.astype(F32), gain).astype(BF16)
+        return mm(frame, wk[...]).astype(BF16), mm(frame, wv[...]).astype(BF16)
+
+    kb[0:tok, :], vb[0:tok, :] = projected(prev[...])
 
     @pl.when(root)
     def _():
@@ -197,15 +221,10 @@
             def _():
                 landed(p)
 
-    sides = layer_norm(side[...].astype(F32).reshape(2 * tok, width), gain).astype(BF16)
-    keys = mm(sides, wk[...]).astype(BF16)
-    values = mm(sides, wv[...]).astype(BF16)
-    ka[...] = keys[0:tok]
-    va[...] = values[0:tok]
-    kb[0:tok, :] = keys[tok:2 * tok]
-    vb[0:tok, :] = values[tok:2 * tok]
+    ka[...], va[...] = projected(anc[...])
 
     loads[4].wait()
+    loads[6].wait()
     c_gain = conv_gain[...].reshape(1, width)
     ones = jnp.ones((2 * tok, PAIR), BF16)
     first_half = lax.broadcasted_iota(jnp.int32, (1, PAIR), 1) < HEAD_DIM
@@ -304,14 +323,6 @@
             to_sibling(t).wait_send()
 
 
-def hand_over(src, out, done):
-    copies = [pltpu.make_async_copy(src.at[0, f], out.at[0, f], done.at[f]) for f in range(src.shape[1])]
-    for c in copies:
-        c.start()
-    for c in copies:
-        c.wait()
-
-
 def solution(mesh):
     nv, nt = mesh.shape["view"], mesh.shape["tm"]
 
@@ -322,14 +333,14 @@
         if not gather:
             conv_weight = lax.all_gather(conv_weight, "tm", axis=0, tiled=True)
         pieces = max(n for n in range(1, nt + 1) if tok % (16 * n) == 0)
-        anywhere = pl.BlockSpec(memory_space=pltpu.HBM)
+        anywhere = pl.BlockSpec(memory_space=pl.ANY)
         vmem = pl.BlockSpec(memory_space=pltpu.VMEM)
         square = pltpu.VMEM((width, width), BF16)
         dma = pltpu.SemaphoreType.DMA
-        block = pl.pallas_call(
+        return pl.pallas_call(
             functools.partial(kernel, nv, nt, pieces, gather),
-            out_shape=pltpu.VMEM(frames.shape, BF16),
-            in_specs=[anywhere, vmem, anywhere, anywhere, anywhere, anywhere, vmem, anywhere],
+            out_shape=jax.ShapeDtypeStruct(frames.shape, BF16),
+            in_specs=[anywhere] * 8,
             out_specs=vmem,
             scratch_shapes=[
                 pltpu.VMEM((nf, tok, width), BF16),
@@ -345,22 +356,16 @@
                 pltpu.VMEM((nf * tok, width), BF16),
                 pltpu.VMEM(((nf + 2) * tok, width), BF16),
                 pltpu.VMEM((3 * width, width), BF16),
-                dma((8,)), dma((pieces,)), dma((nv,)), dma((nt,)), dma((pieces,)),
+                pltpu.VMEM((width,), F32),
+                pltpu.VMEM((width,), F32),
+                dma((10,)), dma((nv, pieces)), dma((nt,)), dma((pieces,)),
                 dma, dma,
                 dma((nt,)), dma((nt,)), dma((nt,)), dma((nt,)), dma((2,)), dma((2,)),
             ],
             compiler_params=pltpu.CompilerParams(
-                collective_id=0, has_side_effects=True, vmem_limit_bytes=48 * 1024 * 1024
+                collective_id=0, has_side_effects=True, vmem_limit_bytes=62 * 1024 * 1024
             ),
         )(frames, ln_gain, w_query, w_key, w_value, w_out, conv_gain, conv_weight)
-        return pl.pallas_call(
-            hand_over,
-            out_shape=jax.ShapeDtypeStruct(frames.shape, BF16),
-            in_specs=[vmem],
-            out_specs=anywhere,
-            scratch_shapes=[dma((nf,))],
-        )(block)
-
     placed = (P("view", "tm", None, None), P(), P(), P(), P(), P(), P(), P("tm", None))
     return jax.shard_map(
         per_device, mesh=mesh, in_specs=placed, out_specs=P("view", "tm", None, None), check_vma=False

time: 48.2 us -> 42.5 us (0.88)
  the two profiles are of different devices: /device:TPU:11 before, /device:TPU:9 now
where the time goes in v3:
time: 42.5 us; the launch traced here: 42.4 us
  Pallas kernels  40.3 us (95%)
  local copies, waits for them, and re-layouts  2.11 us (5%)
    pallas_call x1, Pallas kernels, per_device(): pl.pallas_call(functools.partial(kernel, nv, nt, pieces, gather), out_sha...  40.3 us
    unnamed x1, local copies, waits for them, and re-layouts  2.11 us

profile of v3, /device:TPU:9, one launch (start us, length us, event | category | flops | bytes accessed | tf_op | source)
XLA Modules:
  0.0 42.4 jit_solution(11463321945956474153)
XLA Ops:
  0.0 40.3 %shard_map.82 = bf16[1,4,160,640]{3,2,1,0:T(8,128)(2,1)} custom-call(bf16[1,4,160,640]{3,2,1,0:T(8,128)(2,1)} %fr.1, f32[640]{0:T(1024)} %ln_gain_h.1, bf16[640,640]{1,0:T(8,128)(2,1)} %wq_h.1, bf16[640,640]{1,0:T(8,128)(2,1)} %wk_h.1, bf16[640,640]{1,0:T(8,128)(2,1)} %wv_h.1, bf16[640,640]{1,0:T(8,128)(2,1)} %wo_h.1, f32[640]{0:T(1024)} %conv_gain_h.1, ...), custom_call_target="tpu_custom_call" | custom-call | tf_op jit(solution)/shard_map/pallas_call | solution.py:340
  40.3 2.1 %copy.10 = bf16[1,4,160,640]{3,2,1,0:T(8,128)(2,1)} copy(bf16[1,4,160,640]{3,2,1,0:T(8,128)(2,1)} %shard_map.82) | data formatting | bytes 1638400

commit v4 on v3

--- a/solution.py
+++ b/solution.py
@@ -33,7 +33,7 @@
 def kernel(nv, nt, pieces, gather,
            fr, ln_gain_h, wq_h, wk_h, wv_h, wo_h, conv_gain_h, cw,
            out, x, wq, wk, wv, wo, side, normed, q2, kb, vb, ka, va, att, hid, act, wf, ln_gain, conv_gain,
-           load, s1, s3, ra, sp, rp, sw1, rw1, sw2, rw2, sh, rh):
+           load, s1, s2, s3, ra, sp, rp, sw1, rw1, sw2, rw2, sh, rh):
     v, j = lax.axis_index("view"), lax.axis_index("tm")
     nf, tok, width = x.shape
     part = tok // pieces
@@ -72,29 +72,17 @@
         def _():
             pl.semaphore_signal(barrier, inc=1, device_id=(v, t), device_id_type=MESH)
 
-    @pl.when((v > 0) & (j < pieces))
-    def _():
-        pl.semaphore_signal(barrier, inc=1, device_id=(0, 0), device_id_type=MESH)
-
-    @pl.when(root)
-    def _():
-        @pl.loop(1, nv)
+    @pl.when(j < pieces)
+    def _():
+        @pl.loop(0, nv)
         def _(t):
-            @pl.loop(0, pieces)
-            def _(p):
-                pl.semaphore_signal(barrier, inc=1, device_id=(t, p), device_id_type=MESH)
-
-    far_holder = (v > 0) & (j < pieces)
-
-    @pl.when(root)
-    def _():
-        pl.semaphore_wait(barrier, nt - 1 + (nv - 1) * pieces)
-
-    @pl.when(far_holder)
-    def _():
-        pl.semaphore_wait(barrier, nt)
-
-    @pl.when(jnp.logical_not(root | far_holder))
+            @pl.when(t != v)
+            def _():
+                pl.semaphore_signal(barrier, inc=1, device_id=(t, j), device_id_type=MESH)
+
+        pl.semaphore_wait(barrier, nt - 1 + nv - 1)
+
+    @pl.when(j >= pieces)
     def _():
         pl.semaphore_wait(barrier, nt - 1)
 
@@ -102,6 +90,13 @@
         return pl.ds(pl.multiple_of(p * part, part), part)
 
     def spread(p, src, act_on):
+        @pl.when(v == 0)
+        def _():
+            @pl.loop(1, nv)
+            def _(back):
+                t = nv - back
+                act_on(remote(src, anc.at[rows(p)], s2.at[t], ra.at[p], t, j))
+
         @pl.loop(0, nt)
         def _(t):
             @pl.when((t != j) & ((v != 0) | (t != 0)))
@@ -109,15 +104,9 @@
                 act_on(remote(src, anc.at[rows(p)], s3.at[t], ra.at[p], v, t))
 
     def scatter(act_on):
-        @pl.loop(0, nv)
-        def _(back):
-            t = nv - 1 - back
-
-            @pl.loop(0, pieces)
-            def _(p):
-                @pl.when((t != 0) | (p != 0))
-                def _():
-                    act_on(remote(fr.at[0, 0, rows(p)], anc.at[rows(p)], s1.at[t, p], ra.at[p], t, p))
+        @pl.loop(1, pieces)
+        def _(p):
+            act_on(remote(fr.at[0, 0, rows(p)], anc.at[rows(p)], s1.at[p], ra.at[p], 0, p))
 
     def begin(c):
         c.start()
@@ -153,6 +142,10 @@
     loads[0].wait()
     loads[5].wait()
     gain = ln_gain[...].reshape(1, width)
+
+    @pl.when(holder & (v == 0))
+    def _():
+        forward()
 
     @pl.loop(0, nf)
     def _(f):
@@ -179,7 +172,7 @@
         q2[f, 0:tok, :] = (block * low).astype(BF16)
         q2[f, tok:2 * tok, :] = (block * (1.0 - low)).astype(BF16)
 
-    @pl.when(holder)
+    @pl.when(holder & (v != 0))
     def _():
         forward()
 
@@ -358,7 +351,7 @@
                 pltpu.VMEM((3 * width, width), BF16),
                 pltpu.VMEM((width,), F32),
                 pltpu.VMEM((width,), F32),
-                dma((10,)), dma((nv, pieces)), dma((nt,)), dma((pieces,)),
+                dma((10,)), dma((pieces,)), dma((nv,)), dma((nt,)), dma((pieces,)),
                 dma, dma,
                 dma((nt,)), dma((nt,)), dma((nt,)), dma((nt,)), dma((2,)), dma((2,)),
             ],

time: 42.5 us -> 41.3 us (0.972)
  Pallas kernels: 40.3 us -> 39 us
    pallas_call x1, Pallas kernels: 40.3 us -> 39 us  [per_device(): pl.pallas_call(functools.partial(kernel, nv, nt, pieces, gather), out_sha...]
where the time goes in v4:
time: 41.3 us; the launch traced here: 41.1 us
  Pallas kernels  39 us (94%)
  local copies, waits for them, and re-layouts  2.11 us (5%)
    pallas_call x1, Pallas kernels, per_device(): pl.pallas_call(functools.partial(kernel, nv, nt, pieces, gather), out_sha...  39 us
    unnamed x1, local copies, waits for them, and re-layouts  2.11 us

profile of v4, /device:TPU:9, one launch (start us, length us, event | category | flops | bytes accessed | tf_op | source)
XLA Modules:
  0.0 41.1 jit_solution(3325304543833225415)
XLA Ops:
  0.0 39.0 %shard_map.82 = bf16[1,4,160,640]{3,2,1,0:T(8,128)(2,1)} custom-call(bf16[1,4,160,640]{3,2,1,0:T(8,128)(2,1)} %fr.1, f32[640]{0:T(1024)} %ln_gain_h.1, bf16[640,640]{1,0:T(8,128)(2,1)} %wq_h.1, bf16[640,640]{1,0:T(8,128)(2,1)} %wk_h.1, bf16[640,640]{1,0:T(8,128)(2,1)} %wv_h.1, bf16[640,640]{1,0:T(8,128)(2,1)} %wo_h.1, f32[640]{0:T(1024)} %conv_gain_h.1, ...), custom_call_target="tpu_custom_call" | custom-call | tf_op jit(solution)/shard_map/pallas_call | solution.py:333
  39.0 2.1 %copy.10 = bf16[1,4,160,640]{3,2,1,0:T(8,128)(2,1)} copy(bf16[1,4,160,640]{3,2,1,0:T(8,128)(2,1)} %shard_map.82) | data formatting | bytes 1638400

commit v5 on v4

--- a/solution.py
+++ b/solution.py
@@ -262,22 +262,6 @@
         def _():
             to_left.start()
 
-    @pl.when(j == 0)
-    def _():
-        act[0:tok, :] = jnp.zeros((tok, width), BF16)
-
-    @pl.when(j > 0)
-    def _():
-        to_right.wait_recv()
-
-    @pl.when(j == nt - 1)
-    def _():
-        act[(nf + 1) * tok:(nf + 2) * tok, :] = jnp.zeros((tok, width), BF16)
-
-    @pl.when(j < nt - 1)
-    def _():
-        to_left.wait_recv()
-
     if gather:
         @pl.loop(0, groups)
         def _(t):
@@ -285,9 +269,28 @@
     else:
         own_w.wait()
 
-    total = hid[...].astype(F32)
-    for tap in range(3):
-        total += mm(act[tap * tok:(tap + nf) * tok, :], wf[tap * width:(tap + 1) * width, :])
+    def tapped(tap):
+        return mm(act[tap * tok:(tap + nf) * tok, :], wf[tap * width:(tap + 1) * width, :])
+
+    total = hid[...].astype(F32) + tapped(1)
+
+    @pl.when(j == 0)
+    def _():
+        act[0:tok, :] = jnp.zeros((tok, width), BF16)
+
+    @pl.when(j > 0)
+    def _():
+        to_right.wait_recv()
+
+    @pl.when(j == nt - 1)
+    def _():
+        act[(nf + 1) * tok:(nf + 2) * tok, :] = jnp.zeros((tok, width), BF16)
+
+    @pl.when(j < nt - 1)
+    def _():
+        to_left.wait_recv()
+
+    total += tapped(0) + tapped(2)
     out[...] = total.astype(BF16).reshape(out.shape)
 
     @pl.when(root)

time: 41.3 us -> 40.5 us (0.981)
  Pallas kernels: 39 us -> 38.3 us
    pallas_call x1, Pallas kernels: 39 us -> 38.3 us  [per_device(): pl.pallas_call(functools.partial(kernel, nv, nt, pieces, gather), out_sha...]
where the time goes in v5:
time: 40.5 us; the launch traced here: 40.4 us
  Pallas kernels  38.3 us (95%)
  local copies, waits for them, and re-layouts  2.11 us (5%)
    pallas_call x1, Pallas kernels, per_device(): pl.pallas_call(functools.partial(kernel, nv, nt, pieces, gather), out_sha...  38.3 us
    unnamed x1, local copies, waits for them, and re-layouts  2.11 us

profile of v5, /device:TPU:9, one launch (start us, length us, event | category | flops | bytes accessed | tf_op | source)
XLA Modules:
  0.0 40.4 jit_solution(6345350087418683208)
XLA Ops:
  0.0 38.3 %shard_map.82 = bf16[1,4,160,640]{3,2,1,0:T(8,128)(2,1)} custom-call(bf16[1,4,160,640]{3,2,1,0:T(8,128)(2,1)} %fr.1, f32[640]{0:T(1024)} %ln_gain_h.1, bf16[640,640]{1,0:T(8,128)(2,1)} %wq_h.1, bf16[640,640]{1,0:T(8,128)(2,1)} %wk_h.1, bf16[640,640]{1,0:T(8,128)(2,1)} %wv_h.1, bf16[640,640]{1,0:T(8,128)(2,1)} %wo_h.1, f32[640]{0:T(1024)} %conv_gain_h.1, ...), custom_call_target="tpu_custom_call" | custom-call | tf_op jit(solution)/shard_map/pallas_call | solution.py:336
  38.3 2.1 %copy.10 = bf16[1,4,160,640]{3,2,1,0:T(8,128)(2,1)} copy(bf16[1,4,160,640]{3,2,1,0:T(8,128)(2,1)} %shard_map.82) | data formatting | bytes 1638400
